TPU v7x, 512 devices: a whole 4x4x16 slice. The times are simulated.
512 devices in a mesh: src: 16 (over z), tgt: 32 (over y, x, core).
Axes of the slice: x: 4, y: 4, z: 16, core: 2. Of those that a mesh axis runs over, the one named last changes fastest.
Arguments:
- source_emb: bfloat16 [16384, 1024], P('src', 'tgt'), may hold values from -1100 to 1100
- target_emb: bfloat16 [32768, 1024], P('tgt', 'src'), may hold values from -1100 to 1100
- src_group: int32 [16384], P('src'), may hold values from 0 to 7, as said below
- tgt_group: int32 [32768], P('tgt'), may hold values from 0 to 7, as said below
Outputs:
- margins: float32 [16384, 32768], P('src', 'tgt')
Inputs may be any that keep to these rules, and one draw needn't show every extreme that they name: `src_group`: every block from 0 to 7 labels at least one source sentence. `tgt_group`: every block from 0 to 7 labels at least two target sentences.
All inputs are finite; a program needn't handle non-finite values.
Results may differ from a plain program's by a relative error of at most 0.0003.
Values may be sent and summed in bfloat16 or wider, within the bound.
No kernel may reach another device: no remote copies, remote signals or barrier semaphores. Data moves between devices by JAX's collectives and lax.ppermute only.
A program may use at most 64 MiB of HBM per device.

v0:
```python
import math

import jax
import jax.numpy as jnp
from jax import lax
from jax.sharding import PartitionSpec as P

smoothing_divisor = 256.0
floor_value = -1e30
eps = 1e-06


def inverse_norm(sentences):
    widened_values = sentences.astype(jnp.float32)
    return lax.rsqrt(jnp.sum(widened_values * widened_values, axis=1) + eps)


def pair_level(row_level, col_level):
    highest = jnp.maximum(row_level, col_level)
    return highest + jnp.log1p(jnp.exp(-jnp.abs(row_level - col_level)))


def local(source_emb, target_emb, src_group, tgt_group):
    right_sentence_list = lax.all_gather(target_emb, "src", axis=1, tiled=True)
    right_neighbor_norm = inverse_norm(right_sentence_list)
    sources = lax.all_gather(source_emb, "tgt", axis=1, tiled=True)
    cosine_inner_matrix = lax.dot_general(
        sources, right_sentence_list, (((1,), (1,)), ((), ())), preferred_element_type=jnp.float32
    )
    left_neighbor_norm = inverse_norm(sources)
    bitext_rating_matrix = (
        smoothing_divisor
        * cosine_inner_matrix
        * left_neighbor_norm[:, None]
        * right_neighbor_norm[None, :]
    )
    allowed = src_group[:, None] == tgt_group[None, :]
    weight = allowed.astype(jnp.float32)
    masked_scores = jnp.where(allowed, bitext_rating_matrix, floor_value)
    row_max = jnp.max(masked_scores, axis=1)
    col_max = jnp.max(masked_scores, axis=0)
    row_max = lax.pmax(row_max, "tgt")
    col_max = lax.pmax(col_max, "src")
    row_sum = jnp.sum(weight * jnp.exp(masked_scores - row_max[:, None]), axis=1)
    col_sum = jnp.sum(weight * jnp.exp(masked_scores - col_max[None, :]), axis=0)
    row_sum = lax.psum(row_sum, "tgt")
    col_sum = lax.psum(col_sum, "src")
    row_level = row_max + jnp.log(row_sum)
    col_level = col_max + jnp.log(col_sum)
    margin = (
        bitext_rating_matrix - pair_level(row_level[:, None], col_level[None, :]) + math.log(2.0)
    )
    return jnp.where(allowed, margin, jnp.zeros_like(margin))


def solution(mesh):
    in_specs = (P("src", "tgt"), P("tgt", "src"), P("src"), P("tgt"))
    out_specs = P("src", "tgt")
    return jax.shard_map(local, mesh=mesh, in_specs=in_specs, out_specs=out_specs, check_vma=False)
```

profile of v0, /device:TPU:32, one launch (start us, length us, event | category | flops | bytes accessed | tf_op | source)
XLA Modules:
  0.0 360.7 jit_solution(6344754151435081156)
XLA Ops:
  6.5 0.0 copy-start.1
  6.5 0.0 copy-start.2
  6.5 0.0 all-gather.5.cloned.1.call-start
  6.5 0.7 all-gather.5.cloned.1.call-update
  7.3 0.0 all-gather.3.cloned.1.call-start
  7.3 0.7 all-gather.3.cloned.1.call-update
  8.0 78.8 %all-gather.5.cloned.1.call-done = bf16[1024,1024]{0,1:T(8,128)(2,1)} async-done(((bf16[1024,64]{0,1:T(8,128)(2,1)}), bf16[1024,1024]{0,1:T(8,128)(2,1)}) %all-gather.5.cloned.1.call-update) | async-done | bytes 2097168 | tf_op jit(solution)/shard_map/all_gather | solution.py:24
  86.8 0.0 copy-start
  86.8 2.2 multiply_reduce_fusion
  89.0 56.9 %all-gather.3.cloned.1.call-done = bf16[1024,1024]{0,1:T(8,128)(2,1)} async-done(((bf16[1024,32]{0,1:T(8,128)(2,1)}), bf16[1024,1024]{0,1:T(8,128)(2,1)}) %all-gather.3.cloned.1.call-update) | async-done | bytes 2097168 | tf_op jit(solution)/shard_map/all_gather | solution.py:26
  146.0 2.1 multiply_reduce_fusion.1
  148.0 0.0 copy-done.1
  148.1 0.0 copy-done.2
  148.1 0.0 copy-done
  148.1 6.4 %fusion.3 = (f32[1024]{0:T(1024)S(1)}, f32[1024,1024]{1,0:T(8,128)}) fusion(f32[1024]{0:T(1024)S(1)} %add_rsqrt_fusion, f32[1024]{0:T(1024)S(1)} %rsqrt_multiply_fusion, s32[1024]{0:T(1024)S(1)} %copy-done.1, s32[1024]{0:T(1024)S(1)} %copy-done.2, bf16[1024,1024]{0,1:T(8,128)(2,1)} %all-gather.3.cloned.1.call-done, bf16[1024,1024]{0,1:T(8,128)(2,1)S(1)} %copy-done), kind=kOutput, calls=%fused_computation.14 | convolution fusion | flops 2152725504 | bytes 8409088 | tf_op jit(solution)/shard_map/dot_general | solution.py:27
  154.4 65.2 %pmax.14 = f32[1024]{0:T(1024)S(1)} all-reduce(f32[1024]{0:T(1024)S(1)} %get-tuple-element.7), channel_id=1, replica_groups=mesh['src'=16,'tgt'=32] {'tgt'}, use_global_device_ids=true, to_apply=%region_3.4 | all-reduce | flops 1024 | bytes 8192 | tf_op jit(solution)/shard_map/pmax | solution.py:42
  219.6 3.4 fusion
  223.0 62.7 %psum.14 = f32[1024]{0:T(1024)S(1)} all-reduce(f32[1024]{0:T(1024)S(1)} %get-tuple-element.5), channel_id=1, replica_groups=mesh['src'=16,'tgt'=32] {'tgt'}, use_global_device_ids=true, to_apply=%region_5.6 | all-reduce | flops 1024 | bytes 8192 | tf_op jit(solution)/shard_map/psum | solution.py:46
  285.7 29.9 %pmax.15 = f32[1024]{0:T(1024)S(1)} all-reduce(f32[1024]{0:T(1024)S(1)} %get-tuple-element.6), channel_id=1, replica_groups=mesh['src'=16,'tgt'=32] {'src'}, use_global_device_ids=true, to_apply=%region_7.8 | all-reduce | flops 1024 | bytes 8192 | tf_op jit(solution)/shard_map/pmax | solution.py:43
  315.6 3.0 fusion.1
  318.6 28.9 %psum.15 = f32[1024]{0:T(1024)S(1)} all-reduce(f32[1024]{0:T(1024)S(1)} %fusion.1), channel_id=1, replica_groups=mesh['src'=16,'tgt'=32] {'src'}, use_global_device_ids=true, to_apply=%region_9.10 | all-reduce | flops 1024 | bytes 8192 | tf_op jit(solution)/shard_map/psum | solution.py:47
  347.5 6.3 %compare_select_fusion = f32[1024,1024]{1,0:T(8,128)} fusion(f32[1024,1024]{1,0:T(8,128)} %get-tuple-element.8, f32[1024]{0:T(1024)S(1)} %log_add_fusion, f32[1024]{0:T(1024)S(1)} %log_add_fusion.1, f32[1024]{0:T(1024)S(1)} %add_rsqrt_fusion, f32[1024]{0:T(1024)S(1)} %rsqrt_multiply_fusion, s32[1024]{0:T(1024)S(1)} %copy-done.1, s32[1024]{0:T(1024)S(1)} %copy-done.2), kind=kLoop, calls=%fused_computation | loop fusion | flops 11534336 | bytes 8413184 | tf_op jit(solution)/shard_map/jit(_where)/select_n | solution.py:53
  (4 shorter events, 0.0 us)
Async XLA Ops:
  6.5 141.5 %copy-start.1 = (s32[1024]{0:T(1024)S(1)}, s32[1024]{0:T(1024)}, u32[]{:S(2)}) copy-start(s32[1024]{0:T(1024)} %param.7) | copy-start | bytes 12292
  6.5 141.5 %copy-start.2 = (s32[1024]{0:T(1024)S(1)}, s32[1024]{0:T(1024)}, u32[]{:S(2)}) copy-start(s32[1024]{0:T(1024)} %param.6) | copy-start | bytes 12292
  6.5 80.3 %all-gather.5.cloned.1.call-start = ((), (), s32[]{:S(2)}) async-start(), calls=%async_computation.1 | async-start | bytes 2228224 | tf_op jit(solution)/shard_map/all_gather | solution.py:24
  7.3 138.7 %all-gather.3.cloned.1.call-start = ((), (), s32[]{:S(2)}) async-start(), calls=%async_computation | async-start | bytes 2162688 | tf_op jit(solution)/shard_map/all_gather | solution.py:26
  86.8 61.3 %copy-start = (bf16[1024,1024]{0,1:T(8,128)(2,1)S(1)}, bf16[1024,1024]{0,1:T(8,128)(2,1)}, u32[]{:S(2)}) copy-start(bf16[1024,1024]{0,1:T(8,128)(2,1)} %all-gather.5.cloned.1.call-done) | copy-start | bytes 6291460
Sparse Core Ops, SparseCore 0:
  9.4 77.3 all-gather.4
  89.9 55.9 all-gather.2
where the time goes:
time: 361 us
  blocking collectives  187 us (52%)
  waiting for transfers between devices  137 us (38%)
  other arithmetic  17.1 us (5%)
  between operations  13.4 us (4%)
  matrix products  6.35 us (2%)
    all_gather x1, waiting for transfers between devices, local(): right_sentence_list = lax.all_gather(target_emb, 'src', axis=1, tiled=True)  78.8 us
    pmax x1, blocking collectives, local(): row_max = lax.pmax(row_max, 'tgt')  65.2 us
    psum x1, blocking collectives, local(): row_sum = lax.psum(row_sum, 'tgt')  62.7 us
    all_gather x1, waiting for transfers between devices, local(): sources = lax.all_gather(source_emb, 'tgt', axis=1, tiled=True)  56.9 us
    pmax x1, blocking collectives, local(): col_max = lax.pmax(col_max, 'src')  29.9 us
    psum x1, blocking collectives, local(): col_sum = lax.psum(col_sum, 'src')  28.9 us
  transfers between devices with their start and end apart: 2, of which 2 were waited for; matrix products, arithmetic and copies ran while one was open for 1% of the time, Pallas kernels for 0%

commit v1 on v0

v1 whole, which is shorter than its diff:
```python
import math

import jax
import jax.numpy as jnp
from jax import lax
from jax.experimental import pallas as pl
from jax.experimental.pallas import tpu as pltpu
from jax.sharding import PartitionSpec as P

smoothing_divisor = 256.0
floor_value = -1e30
absent_below = -1e29
eps = 1e-06
lanes = 128


def log_sum_exp(levels):
    highest = jnp.max(levels, axis=0)
    return highest + jnp.log(jnp.sum(jnp.exp(levels - highest[None]), axis=0))


def as_column(line):
    return jnp.transpose(jnp.broadcast_to(line, (lanes, lanes)))


def as_line(column):
    return jnp.transpose(jnp.broadcast_to(column, (lanes, lanes)))[:1]


def score_kernel(pieces, place, *refs):
    source, source_group, target_group = refs[:3]
    piece_refs = refs[3 : 3 + len(pieces)]
    scores, row_out, col_out = refs[3 + len(pieces) : 6 + len(pieces)]
    gathered, scale_cols, group_cols = refs[6 + len(pieces) :]
    z = place[0]
    chunks, depth, columns = gathered.shape
    rows = source.shape[0]
    squares = jnp.zeros((8, columns), jnp.float32)
    for offsets, ref in zip(pieces, piece_refs):
        for k, offset in enumerate(offsets):
            block = ref[k]
            gathered[lax.rem(z + (offset + chunks), chunks)] = block
            wide = block.astype(jnp.float32)
            squares += jnp.sum((wide * wide).reshape(depth // 8, 8, columns), axis=0)
    target_scale = lax.rsqrt(jnp.sum(squares, axis=0, keepdims=True) + eps)

    wide_rows = rows // lanes
    for i in range(wide_rows):
        part = source[pl.ds(i * lanes, lanes), :].astype(jnp.float32)
        norm = lax.rsqrt(jnp.sum(part * part, axis=1, keepdims=True) + eps)
        scale_cols[pl.ds(i * lanes, lanes), :] = jnp.broadcast_to(
            smoothing_divisor * norm, (lanes, lanes)
        )
        group_cols[pl.ds(i * lanes, lanes), :] = as_column(source_group[i : i + 1, :])

    width = 256
    flat = gathered.reshape(chunks * depth, columns)
    target_groups = jnp.concatenate([target_group[i : i + 1, :] for i in range(columns // lanes)], axis=1)
    for n in range(columns // width):
        span = slice(n * width, (n + 1) * width)
        products = jnp.dot(source[...], flat[:, span], preferred_element_type=jnp.float32)
        scaled = products * scale_cols[:, :1] * target_scale[:, span]
        allowed = group_cols[:, :1] == target_groups[:, span]
        scores[:, span] = jnp.where(allowed, scaled, floor_value)

    col_max = jnp.max(scores[...], axis=0, keepdims=True)
    col_sum = jnp.zeros((1, columns), jnp.float32)
    row_lines = []
    for i in range(wide_rows):
        part = scores[pl.ds(i * lanes, lanes), :]
        row_max = jnp.max(part, axis=1, keepdims=True)
        row_sum = jnp.sum(jnp.exp(part - row_max), axis=1, keepdims=True)
        level = jnp.where(row_max < absent_below, floor_value, row_max + jnp.log(row_sum))
        row_lines.append(as_line(level))
        col_sum += jnp.sum(jnp.exp(part - col_max), axis=0, keepdims=True)
    row_out[...] = jnp.concatenate(row_lines, axis=0)
    col_level = jnp.where(col_max < absent_below, floor_value, col_max + jnp.log(col_sum))
    col_out[...] = jnp.concatenate(
        [col_level[:, i * lanes : (i + 1) * lanes] for i in range(columns // lanes)], axis=0
    )


def margin_kernel(scores, row_levels, col_levels, margins, row_column, col_line):
    i = pl.program_id(0)

    @pl.when(i == 0)
    def _():
        rows = log_sum_exp(row_levels[...])
        for k in range(rows.shape[0]):
            row_column[k] = as_column(rows[k : k + 1, :])
        cols = log_sum_exp(col_levels[...])
        col_line[...] = jnp.concatenate([cols[k : k + 1, :] for k in range(cols.shape[0])], axis=1)

    part = scores[...]
    row = row_column[i][:, :1]
    col = col_line[...]
    pair = jnp.maximum(row, col) + jnp.log(1.0 + jnp.exp(-jnp.abs(row - col)))
    margins[...] = jnp.where(part < absent_below, 0.0, part - pair + math.log(2.0))


def local(source_emb, target_emb, src_group, tgt_group):
    z_size = lax.axis_size("src")
    t_size = lax.axis_size("tgt")

    def shift(x, step):
        return lax.ppermute(x, "src", [(i, (i + step) % z_size) for i in range(z_size)])

    own = target_emb.T
    low, high = shift(own, 5), shift(own, -5)
    three = jnp.stack([own, low, high])
    one, mone = shift(three, 1), shift(three, -1)
    two, mtwo = shift(three, 2), shift(three, -2)
    far = shift(low, 3)
    pieces = [
        ((0, -5, 5), three),
        ((-1, -6, 4), one),
        ((1, -4, 6), mone),
        ((-2, -7, 3), two),
        ((2, -3, 7), mtwo),
        ((-8,), far[None]),
    ]
    part = source_emb.T
    sources = lax.all_to_all(jnp.broadcast_to(part[None], (t_size,) + part.shape), "tgt", 0, 0)
    sources = sources.reshape(-1, sources.shape[-1]).T

    rows, columns, chunks = sources.shape[0], own.shape[1], z_size
    place = lax.axis_index("src").astype(jnp.int32).reshape(1)
    vmem = pl.BlockSpec(memory_space=pltpu.VMEM)
    scores, row_level, col_level = pl.pallas_call(
        lambda *refs: score_kernel([p for p, _ in pieces], *refs),
        out_shape=(
            jax.ShapeDtypeStruct((rows, columns), jnp.float32),
            jax.ShapeDtypeStruct((rows // lanes, lanes), jnp.float32),
            jax.ShapeDtypeStruct((columns // lanes, lanes), jnp.float32),
        ),
        in_specs=[pl.BlockSpec(memory_space=pltpu.SMEM)] + [vmem] * (3 + len(pieces)),
        out_specs=(vmem, vmem, vmem),
        scratch_shapes=[
            pltpu.VMEM((chunks, own.shape[0], columns), jnp.bfloat16),
            pltpu.VMEM((rows, lanes), jnp.float32),
            pltpu.VMEM((rows, lanes), jnp.int32),
        ],
        compiler_params=pltpu.CompilerParams(vmem_limit_bytes=48 * 2**20),
        name="scores",
    )(place, sources, src_group.reshape(-1, lanes), tgt_group.reshape(-1, lanes), *[x for _, x in pieces])

    col_levels = lax.all_to_all(jnp.broadcast_to(col_level[None], (z_size,) + col_level.shape), "src", 0, 0)
    row_levels = lax.all_to_all(jnp.broadcast_to(row_level[None], (t_size,) + row_level.shape), "tgt", 0, 0)

    return pl.pallas_call(
        margin_kernel,
        grid=(rows // lanes,),
        out_shape=jax.ShapeDtypeStruct((rows, columns), jnp.float32),
        in_specs=[
            pl.BlockSpec((lanes, columns), lambda i: (i, 0)),
            pl.BlockSpec(row_levels.shape, lambda i: (0, 0, 0)),
            pl.BlockSpec(col_levels.shape, lambda i: (0, 0, 0)),
        ],
        out_specs=pl.BlockSpec((lanes, columns), lambda i: (i, 0)),
        scratch_shapes=[
            pltpu.VMEM((rows // lanes, lanes, lanes), jnp.float32),
            pltpu.VMEM((1, columns), jnp.float32),
        ],
        compiler_params=pltpu.CompilerParams(vmem_limit_bytes=32 * 2**20),
        name="margins",
    )(scores, row_levels, col_levels)


def solution(mesh):
    in_specs = (P("src", "tgt"), P("tgt", "src"), P("src"), P("tgt"))
    out_specs = P("src", "tgt")
    return jax.shard_map(local, mesh=mesh, in_specs=in_specs, out_specs=out_specs, check_vma=False)
```

time: 361 us -> 138 us (0.38)
  the two profiles are of different devices: /device:TPU:32 before, /device:TPU:1 now
where the time goes in v1:
time: 138 us; the launch traced here: 137 us
  starting transfers between devices  45.2 us (33%)
  blocking collectives  42.1 us (31%)
  waiting for transfers between devices  29.5 us (21%)
  Pallas kernels  11.6 us (8%)
  local copies, waits for them, and re-layouts  8.83 us (6%)
    ppermute x7, starting transfers between devices, shift(): lax.ppermute(x, 'src', [(i, (i + step) % z_size) for i in range(z_size)])  34.6 us
    ppermute x7, waiting for transfers between devices, shift(): lax.ppermute(x, 'src', [(i, (i + step) % z_size) for i in range(z_size)])  29.5 us
    all_to_all x1, blocking collectives, local(): lax.all_to_all(jnp.broadcast_to(col_level[None], (z_size,) + col_level.sh...  22.2 us
    all_to_all x1, blocking collectives, local(): lax.all_to_all(jnp.broadcast_to(row_level[None], (t_size,) + row_level.sh...  19.8 us
    all_to_all x1, starting transfers between devices, local(): lax.all_to_all(jnp.broadcast_to(part[None], (t_size,) + part.shape), 'tgt...  10.7 us
    pallas_call x1, Pallas kernels, local(): pl.pallas_call(lambda *refs: score_kernel([p for p, _ in pieces], *refs),...  6.55 us
    pallas_call x1, Pallas kernels, local(): pl.pallas_call(margin_kernel, grid=(rows // lanes,), out_shape=jax.ShapeD...  5.02 us
    unnamed x10, local copies, waits for them, and re-layouts  3.51 us
  transfers between devices with their start and end apart: 8, of which 4 were waited for; matrix products, arithmetic and copies ran while one was open for 2% of the time, Pallas kernels for 0%

profile of v1, /device:TPU:1, one launch (start us, length us, event | category | flops | bytes accessed | tf_op | source)
XLA Modules:
  0.0 137.4 jit_solution(17457864137545928566)
XLA Ops:
  0.0 2.4 %broadcast_in_dim.8 = bf16[32,32,1024]{2,1,0:T(8,128)(2,1)} broadcast(bf16[32,1024]{1,0:T(8,128)(2,1)} %bitcast.22), dimensions={1,2} | broadcast | bytes 2162688 | tf_op jit(solution)/shard_map/broadcast_in_dim | solution.py:123
  2.4 10.7 %all-to-all-start = ((bf16[32,32,1024]{2,1,0:T(8,128)(2,1)}), bf16[32,32,1024]{2,1,0:T(8,128)(2,1)S(1)}, u32[]{:S(2)}, u32[]{:S(2)}) async-start(bf16[32,32,1024]{2,1,0:T(8,128)(2,1)} %broadcast_in_dim.8), calls=%async_computation | async-start | bytes 4194304 | tf_op jit(solution)/shard_map/all_to_all | solution.py:123
  13.1 8.2 %collective-permute-start = (bf16[64,1024]{1,0:T(8,128)(2,1)S(1)}, bf16[64,1024]{1,0:T(8,128)(2,1)S(1)}, u32[]{:S(2)}, u32[]{:S(2)}) collective-permute-start(bf16[64,1024]{1,0:T(8,128)(2,1)S(1)} %bitcast.17), channel_id=1, source_target_pairs={{0,160},{32,192},{64,224},{96,256},{128,288},{160,320},{192,352},{... | collective-permute-start | bytes 393224 | tf_op jit(solution)/shard_map/ppermute | solution.py:106
  21.3 5.9 %collective-permute-start.1 = (bf16[64,1024]{1,0:T(8,128)(2,1)S(1)}, bf16[64,1024]{1,0:T(8,128)(2,1)S(1)}, u32[]{:S(2)}, u32[]{:S(2)}) collective-permute-start(bf16[64,1024]{1,0:T(8,128)(2,1)S(1)} %bitcast.18), channel_id=1, source_target_pairs={{0,352},{32,384},{64,416},{96,448},{128,480},{160,0},{192,32},{224... | collective-permute-start | bytes 393224 | tf_op jit(solution)/shard_map/ppermute | solution.py:106
  27.2 1.9 %collective-permute-done = bf16[64,1024]{1,0:T(8,128)(2,1)S(1)} collective-permute-done((bf16[64,1024]{1,0:T(8,128)(2,1)S(1)}, bf16[64,1024]{1,0:T(8,128)(2,1)S(1)}, u32[]{:S(2)}, u32[]{:S(2)}) %collective-permute-start) | collective-permute-done | bytes 131104 | tf_op jit(solution)/shard_map/ppermute | solution.py:106
  29.1 12.2 %collective-permute-done.1 = bf16[64,1024]{1,0:T(8,128)(2,1)S(1)} collective-permute-done((bf16[64,1024]{1,0:T(8,128)(2,1)S(1)}, bf16[64,1024]{1,0:T(8,128)(2,1)S(1)}, u32[]{:S(2)}, u32[]{:S(2)}) %collective-permute-start.1) | collective-permute-done | bytes 131104 | tf_op jit(solution)/shard_map/ppermute | solution.py:106
  41.3 4.7 %collective-permute-start.5 = (bf16[3,64,1024]{2,1,0:T(8,128)(2,1)S(1)}, bf16[3,64,1024]{2,1,0:T(8,128)(2,1)S(1)}, u32[]{:S(2)}, u32[]{:S(2)}) collective-permute-start(bf16[3,64,1024]{2,1,0:T(8,128)(2,1)S(1)} %pad_maximum_fusion.refs_4_), channel_id=1, source_target_pairs={{0,448},{32,480},{64,0},{96,32},{128,64},{160,96},{192,128},{224,1... | collective-permute-start | bytes 1179656 | tf_op jit(solution)/shard_map/ppermute | solution.py:106
  46.1 1.9 %collective-permute-start.4 = (bf16[3,64,1024]{2,1,0:T(8,128)(2,1)S(1)}, bf16[3,64,1024]{2,1,0:T(8,128)(2,1)S(1)}, u32[]{:S(2)}, u32[]{:S(2)}) collective-permute-start(bf16[3,64,1024]{2,1,0:T(8,128)(2,1)S(1)} %pad_maximum_fusion.refs_4_), channel_id=1, source_target_pairs={{0,64},{32,96},{64,128},{96,160},{128,192},{160,224},{192,256},{22... | collective-permute-start | bytes 1179656 | tf_op jit(solution)/shard_map/ppermute | solution.py:106
  48.0 6.9 %collective-permute-start.3 = (bf16[3,64,1024]{2,1,0:T(8,128)(2,1)S(1)}, bf16[3,64,1024]{2,1,0:T(8,128)(2,1)}, u32[]{:S(2)}, u32[]{:S(2)}) collective-permute-start(bf16[3,64,1024]{2,1,0:T(8,128)(2,1)S(1)} %pad_maximum_fusion.refs_4_), channel_id=1, source_target_pairs={{0,480},{32,0},{64,32},{96,64},{128,96},{160,128},{192,160},{224,1... | collective-permute-start | bytes 1179656 | tf_op jit(solution)/shard_map/ppermute | solution.py:106
  54.9 1.9 %collective-permute-start.2 = (bf16[3,64,1024]{2,1,0:T(8,128)(2,1)S(1)}, bf16[3,64,1024]{2,1,0:T(8,128)(2,1)}, u32[]{:S(2)}, u32[]{:S(2)}) collective-permute-start(bf16[3,64,1024]{2,1,0:T(8,128)(2,1)S(1)} %pad_maximum_fusion.refs_4_), channel_id=1, source_target_pairs={{0,32},{32,64},{64,96},{96,128},{128,160},{160,192},{192,224},{224... | collective-permute-start | bytes 1179656 | tf_op jit(solution)/shard_map/ppermute | solution.py:106
  56.8 5.1 %collective-permute-start.6 = (bf16[64,1024]{1,0:T(8,128)(2,1)S(1)}, bf16[64,1024]{1,0:T(8,128)(2,1)S(1)}, u32[]{:S(2)}, u32[]{:S(2)}) collective-permute-start(bf16[64,1024]{1,0:T(8,128)(2,1)S(1)} %collective-permute-done), channel_id=1, source_target_pairs={{0,96},{32,128},{64,160},{96,192},{128,224},{160,256},{192,288},{2... | collective-permute-start | bytes 393224 | tf_op jit(solution)/shard_map/ppermute | solution.py:106
  61.9 0.0 all-to-all-done
  61.9 0.0 copy-start.3
  61.9 1.3 copy-done.3
  63.2 2.9 %copy.6 = bf16[1024,1024]{0,1:T(8,128)(2,1)S(1)} copy(bf16[1024,1024]{1,0:T(8,128)(2,1)} %bitcast.16) | data formatting | bytes 4194304 | tf_op jit(solution)/shard_map/reshape | solution.py:124
  66.1 13.2 %collective-permute-done.6 = bf16[64,1024]{1,0:T(8,128)(2,1)S(1)} collective-permute-done((bf16[64,1024]{1,0:T(8,128)(2,1)S(1)}, bf16[64,1024]{1,0:T(8,128)(2,1)S(1)}, u32[]{:S(2)}, u32[]{:S(2)}) %collective-permute-start.6) | collective-permute-done | bytes 131104 | tf_op jit(solution)/shard_map/ppermute | solution.py:106
  79.3 0.0 collective-permute-done.5.refs_8_
  79.3 0.0 collective-permute-done.4.refs_7_
  79.3 2.2 %collective-permute-done.2.refs_5_ = bf16[3,64,1024]{2,1,0:T(8,128)(2,1)} collective-permute-done((bf16[3,64,1024]{2,1,0:T(8,128)(2,1)S(1)}, bf16[3,64,1024]{2,1,0:T(8,128)(2,1)}, u32[]{:S(2)}, u32[]{:S(2)}) %collective-permute-start.2) | collective-permute-done | bytes 393248 | tf_op jit(solution)/shard_map/ppermute | solution.py:106
  81.5 6.5 %scores.1 = (f32[1024,1024]{1,0:T(8,128)}, f32[8,128]{1,0:T(8,128)S(1)}, f32[8,128]{1,0:T(8,128)S(1)}) custom-call(s32[1]{0:T(128)} %bitcast.refs_0_, bf16[1024,1024]{1,0:T(8,128)(2,1)S(1)} %bitcast.12, s32[8,128]{1,0:T(8,128)S(1)} %bitcast.14, s32[8,128]{1,0:T(8,128)S(1)} %bitcast.15, bf16[3,64,1024]{2,1,0:T(8,128)(2,1)S(1)} %pad_maximum_fusion.refs_4_, ...), custom_call_target="tpu_custom_call" | custom-call | tf_op jit(solution)/shard_map/scores/pallas_call | solution.py:129
  88.1 19.8 %all_to_all.15.row_levels = f32[32,8,128]{2,1,0:T(8,128)S(1)} all-to-all(f32[32,8,128]{2,1,0:T(8,128)S(1)} %broadcast_in_dim.10), channel_id=1, replica_groups=mesh['src'=16,'tgt'=32] {'tgt'}, dimensions={0} | all-to-all | bytes 262144 | tf_op jit(solution)/shard_map/all_to_all | solution.py:148
  107.9 22.2 %all_to_all.16.col_levels = f32[16,8,128]{2,1,0:T(8,128)S(1)} all-to-all(f32[16,8,128]{2,1,0:T(8,128)S(1)} %broadcast_in_dim.11), channel_id=1, replica_groups=mesh['src'=16,'tgt'=32] {'src'}, dimensions={0} | all-to-all | bytes 131072 | tf_op jit(solution)/shard_map/all_to_all | solution.py:147
  130.1 2.2 %copy-done = f32[1024,1024]{1,0:T(8,128)S(1)} copy-done((f32[1024,1024]{1,0:T(8,128)S(1)}, f32[1024,1024]{1,0:T(8,128)}, u32[]{:S(2)}) %copy-start) | copy-done | bytes 4194328
  132.3 5.0 %margins.1 = f32[1024,1024]{1,0:T(8,128)} custom-call(f32[1024,1024]{1,0:T(8,128)S(1)} %copy-done, f32[32,8,128]{2,1,0:T(8,128)S(1)} %all_to_all.15.row_levels, f32[16,8,128]{2,1,0:T(8,128)S(1)} %all_to_all.16.col_levels), custom_call_target="tpu_custom_call" | custom-call | tf_op jit(solution)/shard_map/margins/pallas_call | solution.py:150
  (11 shorter events, 0.1 us)
Async XLA Ops:
  2.4 10.7 %copy-start.4 = (bf16[1024,64]{0,1:T(8,128)(2,1)S(1)}, bf16[1024,64]{0,1:T(8,128)(2,1)}, u32[]{:S(2)}) copy-start(bf16[1024,64]{0,1:T(8,128)(2,1)} %param.5) | copy-start | bytes 393220
  2.4 59.5 %all-to-all-start = ((bf16[32,32,1024]{2,1,0:T(8,128)(2,1)}), bf16[32,32,1024]{2,1,0:T(8,128)(2,1)S(1)}, u32[]{:S(2)}, u32[]{:S(2)}) async-start(bf16[32,32,1024]{2,1,0:T(8,128)(2,1)} %broadcast_in_dim.8), calls=%async_computation | async-start | bytes 4194304 | tf_op jit(solution)/shard_map/all_to_all | solution.py:123
  13.1 16.0 %collective-permute-start = (bf16[64,1024]{1,0:T(8,128)(2,1)S(1)}, bf16[64,1024]{1,0:T(8,128)(2,1)S(1)}, u32[]{:S(2)}, u32[]{:S(2)}) collective-permute-start(bf16[64,1024]{1,0:T(8,128)(2,1)S(1)} %bitcast.17), channel_id=1, source_target_pairs={{0,160},{32,192},{64,224},{96,256},{128,288},{160,320},{192,352},{... | collective-permute-start | bytes 393224 | tf_op jit(solution)/shard_map/ppermute | solution.py:106
  21.3 20.0 %collective-permute-start.1 = (bf16[64,1024]{1,0:T(8,128)(2,1)S(1)}, bf16[64,1024]{1,0:T(8,128)(2,1)S(1)}, u32[]{:S(2)}, u32[]{:S(2)}) collective-permute-start(bf16[64,1024]{1,0:T(8,128)(2,1)S(1)} %bitcast.18), channel_id=1, source_target_pairs={{0,352},{32,384},{64,416},{96,448},{128,480},{160,0},{192,32},{224... | collective-permute-start | bytes 393224 | tf_op jit(solution)/shard_map/ppermute | solution.py:106
  41.3 38.0 %collective-permute-start.5 = (bf16[3,64,1024]{2,1,0:T(8,128)(2,1)S(1)}, bf16[3,64,1024]{2,1,0:T(8,128)(2,1)S(1)}, u32[]{:S(2)}, u32[]{:S(2)}) collective-permute-start(bf16[3,64,1024]{2,1,0:T(8,128)(2,1)S(1)} %pad_maximum_fusion.refs_4_), channel_id=1, source_target_pairs={{0,448},{32,480},{64,0},{96,32},{128,64},{160,96},{192,128},{224,1... | collective-permute-start | bytes 1179656 | tf_op jit(solution)/shard_map/ppermute | solution.py:106
  46.1 33.2 %collective-permute-start.4 = (bf16[3,64,1024]{2,1,0:T(8,128)(2,1)S(1)}, bf16[3,64,1024]{2,1,0:T(8,128)(2,1)S(1)}, u32[]{:S(2)}, u32[]{:S(2)}) collective-permute-start(bf16[3,64,1024]{2,1,0:T(8,128)(2,1)S(1)} %pad_maximum_fusion.refs_4_), channel_id=1, source_target_pairs={{0,64},{32,96},{64,128},{96,160},{128,192},{160,224},{192,256},{22... | collective-permute-start | bytes 1179656 | tf_op jit(solution)/shard_map/ppermute | solution.py:106
  48.0 31.3 %collective-permute-start.3 = (bf16[3,64,1024]{2,1,0:T(8,128)(2,1)S(1)}, bf16[3,64,1024]{2,1,0:T(8,128)(2,1)}, u32[]{:S(2)}, u32[]{:S(2)}) collective-permute-start(bf16[3,64,1024]{2,1,0:T(8,128)(2,1)S(1)} %pad_maximum_fusion.refs_4_), channel_id=1, source_target_pairs={{0,480},{32,0},{64,32},{96,64},{128,96},{160,128},{192,160},{224,1... | collective-permute-start | bytes 1179656 | tf_op jit(solution)/shard_map/ppermute | solution.py:106
  54.9 26.6 %collective-permute-start.2 = (bf16[3,64,1024]{2,1,0:T(8,128)(2,1)S(1)}, bf16[3,64,1024]{2,1,0:T(8,128)(2,1)}, u32[]{:S(2)}, u32[]{:S(2)}) collective-permute-start(bf16[3,64,1024]{2,1,0:T(8,128)(2,1)S(1)} %pad_maximum_fusion.refs_4_), channel_id=1, source_target_pairs={{0,32},{32,64},{64,96},{96,128},{128,160},{160,192},{192,224},{224... | collective-permute-start | bytes 1179656 | tf_op jit(solution)/shard_map/ppermute | solution.py:106
  56.8 22.5 %collective-permute-start.6 = (bf16[64,1024]{1,0:T(8,128)(2,1)S(1)}, bf16[64,1024]{1,0:T(8,128)(2,1)S(1)}, u32[]{:S(2)}, u32[]{:S(2)}) collective-permute-start(bf16[64,1024]{1,0:T(8,128)(2,1)S(1)} %collective-permute-done), channel_id=1, source_target_pairs={{0,96},{32,128},{64,160},{96,192},{128,224},{160,256},{192,288},{2... | collective-permute-start | bytes 393224 | tf_op jit(solution)/shard_map/ppermute | solution.py:106
  61.9 1.3 copy-start.3
  63.2 18.3 %copy-start.1 = (s32[1024]{0:T(1024)S(1)}, s32[1024]{0:T(1024)}, u32[]{:S(2)}) copy-start(s32[1024]{0:T(1024)} %param.6) | copy-start | bytes 12292
  63.2 18.3 %copy-start.2 = (s32[1024]{0:T(1024)S(1)}, s32[1024]{0:T(1024)}, u32[]{:S(2)}) copy-start(s32[1024]{0:T(1024)} %param.7) | copy-start | bytes 12292
  130.1 2.2 %copy-start = (f32[1024,1024]{1,0:T(8,128)S(1)}, f32[1024,1024]{1,0:T(8,128)}, u32[]{:S(2)}) copy-start(f32[1024,1024]{1,0:T(8,128)} %get-tuple-element.8.scores) | copy-start | bytes 12582916

commit v2 on v1

v2 whole, which is shorter than its diff:
```python
import math

import jax
import jax.numpy as jnp
from jax import lax
from jax.experimental import pallas as pl
from jax.experimental.pallas import tpu as pltpu
from jax.sharding import PartitionSpec as P

smoothing_divisor = 256.0
floor_value = -1e30
absent_below = -1e29
eps = 1e-06
lanes = 128
code_scale = 512.0


def encode(x):
    wide = x.astype(jnp.float32)
    root = jnp.sqrt(jnp.abs(wide)) * code_scale
    return jnp.where(wide < 0, -root, root).astype(jnp.float16)


def decode(code):
    wide = code.astype(jnp.float32)
    return (wide * jnp.abs(wide) * (1.0 / code_scale**2)).astype(jnp.bfloat16)


def log_sum_exp(levels):
    highest = jnp.max(levels, axis=0)
    return highest + jnp.log(jnp.sum(jnp.exp(levels - highest[None]), axis=0))


def as_column(line):
    return jnp.transpose(jnp.broadcast_to(line, (lanes, lanes)))


def as_line(column):
    return jnp.transpose(jnp.broadcast_to(column, (lanes, lanes)))[:1]


def inverse_norm(features):
    depth, count = features.shape
    squares = jnp.zeros((8, count), jnp.float32)
    step = 64
    for k in range(0, depth, step):
        wide = features[k : k + step, :].astype(jnp.float32)
        squares += jnp.sum((wide * wide).reshape(step // 8, 8, count), axis=0)
    return lax.rsqrt(jnp.sum(squares, axis=0, keepdims=True) + eps)


def score_kernel(source, target, source_group, target_group, scores, row_out, col_out, turned, scale_cols, group_cols):
    depth, rows = source.shape
    columns = target.shape[1]
    target_scale = inverse_norm(target)
    source_scale = inverse_norm(source) * smoothing_divisor
    for i in range(rows // lanes):
        block = slice(i * lanes, (i + 1) * lanes)
        scale_cols[block, :] = as_column(source_scale[:, block])
        group_cols[block, :] = as_column(source_group[i : i + 1, :])
        turned[block, :] = jnp.transpose(source[:, block])

    width = 256
    target_groups = jnp.concatenate([target_group[i : i + 1, :] for i in range(columns // lanes)], axis=1)
    for n in range(columns // width):
        span = slice(n * width, (n + 1) * width)
        products = jnp.dot(turned[...], target[:, span], preferred_element_type=jnp.float32)
        scaled = products * scale_cols[:, :1] * target_scale[:, span]
        allowed = group_cols[:, :1] == target_groups[:, span]
        scores[:, span] = jnp.where(allowed, scaled, floor_value)

    col_max = jnp.max(scores[...], axis=0, keepdims=True)
    col_sum = jnp.zeros((1, columns), jnp.float32)
    row_lines = []
    for i in range(rows // lanes):
        part = scores[i * lanes : (i + 1) * lanes, :]
        row_max = jnp.max(part, axis=1, keepdims=True)
        row_sum = jnp.sum(jnp.exp(part - row_max), axis=1, keepdims=True)
        level = jnp.where(row_max < absent_below, floor_value, row_max + jnp.log(row_sum))
        row_lines.append(as_line(level))
        col_sum += jnp.sum(jnp.exp(part - col_max), axis=0, keepdims=True)
    row_out[...] = jnp.concatenate(row_lines, axis=0)
    col_level = jnp.where(col_max < absent_below, floor_value, col_max + jnp.log(col_sum))
    col_out[...] = jnp.concatenate(
        [col_level[:, i * lanes : (i + 1) * lanes] for i in range(columns // lanes)], axis=0
    )


def margin_kernel(scores, row_levels, col_levels, margins, row_column, col_line):
    i = pl.program_id(0)

    @pl.when(i == 0)
    def _():
        rows = log_sum_exp(row_levels[...])
        for k in range(rows.shape[0]):
            row_column[k] = as_column(rows[k : k + 1, :])
        cols = log_sum_exp(col_levels[...])
        col_line[...] = jnp.concatenate([cols[k : k + 1, :] for k in range(cols.shape[0])], axis=1)

    part = scores[pl.ds(pl.multiple_of(i * lanes, lanes), lanes), :]
    row = row_column[i][:, :1]
    col = col_line[...]
    pair = jnp.maximum(row, col) + jnp.log(1.0 + jnp.exp(-jnp.abs(row - col)))
    margins[...] = jnp.where(part < absent_below, 0.0, part - pair + math.log(2.0))


def find_scores(source, target, src_group, tgt_group):
    rows, columns = source.shape[1], target.shape[1]
    vmem = pl.BlockSpec(memory_space=pltpu.VMEM)
    return pl.pallas_call(
        score_kernel,
        out_shape=(
            jax.ShapeDtypeStruct((rows, columns), jnp.float32),
            jax.ShapeDtypeStruct((rows // lanes, lanes), jnp.float32),
            jax.ShapeDtypeStruct((columns // lanes, lanes), jnp.float32),
        ),
        in_specs=[vmem] * 4,
        out_specs=(vmem, vmem, vmem),
        scratch_shapes=[
            pltpu.VMEM((rows, source.shape[0]), jnp.bfloat16),
            pltpu.VMEM((rows, lanes), jnp.float32),
            pltpu.VMEM((rows, lanes), jnp.int32),
        ],
        compiler_params=pltpu.CompilerParams(vmem_limit_bytes=48 * 2**20),
        name="scores",
    )(source, target, src_group.reshape(-1, lanes), tgt_group.reshape(-1, lanes))


def find_margins(scores, row_levels, col_levels):
    rows, columns = scores.shape
    vmem = pl.BlockSpec(memory_space=pltpu.VMEM)
    return pl.pallas_call(
        margin_kernel,
        grid=(rows // lanes,),
        out_shape=jax.ShapeDtypeStruct((rows, columns), jnp.float32),
        in_specs=[vmem, vmem, vmem],
        out_specs=pl.BlockSpec((lanes, columns), lambda i: (i, 0)),
        scratch_shapes=[
            pltpu.VMEM((rows // lanes, lanes, lanes), jnp.float32),
            pltpu.VMEM((1, columns), jnp.float32),
        ],
        compiler_params=pltpu.CompilerParams(vmem_limit_bytes=32 * 2**20),
        name="margins",
    )(scores, row_levels, col_levels)


def local(source_emb, target_emb, src_group, tgt_group):
    z_size = lax.axis_size("src")
    t_size = lax.axis_size("tgt")
    part = source_emb.T
    source = lax.all_to_all(jnp.broadcast_to(part[None], (t_size,) + part.shape), "tgt", 0, 0)
    source = source.reshape(-1, source.shape[-1])
    target = decode(lax.all_gather(encode(target_emb.T), "src", axis=0, tiled=True))
    scores, row_level, col_level = find_scores(source, target, src_group, tgt_group)
    col_levels = lax.all_to_all(jnp.broadcast_to(col_level[None], (z_size,) + col_level.shape), "src", 0, 0)
    row_levels = lax.all_to_all(jnp.broadcast_to(row_level[None], (t_size,) + row_level.shape), "tgt", 0, 0)
    return find_margins(scores, row_levels, col_levels)


def solution(mesh):
    in_specs = (P("src", "tgt"), P("tgt", "src"), P("src"), P("tgt"))
    out_specs = P("src", "tgt")
    return jax.shard_map(local, mesh=mesh, in_specs=in_specs, out_specs=out_specs, check_vma=False)
```

time: 138 us -> 111 us (0.80)
  blocking collectives: 42.1 us -> 80.7 us
  starting transfers between devices: 45.2 us -> 10.5 us
  waiting for transfers between devices: 29.5 us -> 0.01 us
  local copies, waits for them, and re-layouts: 8.83 us -> 6.26 us
  other arithmetic: 0.05 us -> 2.17 us
    all_gather x0 -> x1, blocking collectives: none -> 42 us  [local(): lax.all_gather(encode(target_emb.T), 'src', axis=0, tiled=True)]
    ppermute x7 -> x0, starting transfers between devices: 34.6 us -> none  [shift(): lax.ppermute(x, 'src', [(i, (i + step) % z_size) for i in range(z_size)])]
    ppermute x7 -> x0, waiting for transfers between devices: 29.5 us -> none  [shift(): lax.ppermute(x, 'src', [(i, (i + step) % z_size) for i in range(z_size)])]
    all_to_all x1, blocking collectives: 22.2 us -> 17.9 us  [local(): lax.all_to_all(jnp.broadcast_to(col_level[None], (z_size,) + col_level.sh...]
    reshape x1 -> x0, local copies, waits for them, and re-layouts: 2.88 us -> none  [local(): sources = sources.reshape(-1, sources.shape[-1]).T]
    convert_element_type x0 -> x2, other arithmetic: none -> 2.17 us  [the longest x1 2.04 us: decode(): return (wide * jnp.abs(wide) * (1.0 / code_scale ** 2)).astype(jnp.bfloat16)]
  transfers between devices with their start and end apart: 8 -> 1, of which waited for: 4 -> 0; matrix products, arithmetic and copies ran while one was open for 2% -> 2% of each run, Pallas kernels for 0% -> 0%
where the time goes in v2:
time: 111 us
  blocking collectives  80.7 us (73%)
  Pallas kernels  10.9 us (10%)
  starting transfers between devices  10.5 us (9%)
  local copies, waits for them, and re-layouts  6.26 us (6%)
  other arithmetic  2.17 us (2%)
    all_gather x1, blocking collectives, local(): lax.all_gather(encode(target_emb.T), 'src', axis=0, tiled=True)  42 us
    all_to_all x1, blocking collectives, local(): lax.all_to_all(jnp.broadcast_to(row_level[None], (t_size,) + row_level.sh...  20.8 us
    all_to_all x1, blocking collectives, local(): lax.all_to_all(jnp.broadcast_to(col_level[None], (z_size,) + col_level.sh...  17.9 us
    all_to_all x1, starting transfers between devices, local(): lax.all_to_all(jnp.broadcast_to(part[None], (t_size,) + part.shape), 'tgt...  10.5 us
    pallas_call x1, Pallas kernels, find_scores(): pl.pallas_call(score_kernel, out_shape=(jax.ShapeDtypeStruct((rows, colum...  5.88 us
    pallas_call x1, Pallas kernels, find_margins(): pl.pallas_call(margin_kernel, grid=(rows // lanes,), out_shape=jax.ShapeD...  5.02 us
    unnamed x10, local copies, waits for them, and re-layouts  3.79 us
    broadcast_in_dim x1, local copies, waits for them, and re-layouts, local(): jnp.broadcast_to(part[None], (t_size,) + part.shape)  2.45 us
  transfers between devices with their start and end apart: 1, of which 0 were waited for; matrix products, arithmetic and copies ran while one was open for 2% of the time, Pallas kernels for 0%

profile of v2, /device:TPU:1, one launch (start us, length us, event | category | flops | bytes accessed | tf_op | source)
XLA Modules:
  0.0 110.6 jit_solution(2295100165764368993)
XLA Ops:
  0.0 0.0 copy-start.4
  0.0 2.5 %broadcast_in_dim.6 = bf16[32,32,1024]{2,1,0:T(8,128)(2,1)} broadcast(bf16[32,1024]{1,0:T(8,128)(2,1)} %bitcast.17), dimensions={1,2} | broadcast | bytes 2162688 | tf_op jit(solution)/shard_map/broadcast_in_dim | solution.py:151
  2.5 10.5 %all-to-all-start = ((bf16[32,32,1024]{2,1,0:T(8,128)(2,1)}), bf16[32,32,1024]{2,1,0:T(8,128)(2,1)S(1)}, u32[]{:S(2)}, u32[]{:S(2)}) async-start(bf16[32,32,1024]{2,1,0:T(8,128)(2,1)} %broadcast_in_dim.6), calls=%async_computation | async-start | bytes 4194304 | tf_op jit(solution)/shard_map/all_to_all | solution.py:151
  13.0 0.0 copy-done.4
  13.0 0.0 copy-start.2
  13.0 0.0 copy-start.3
  13.0 0.1 fusion.5
  13.2 42.0 %all-gather.1 = f16[1024,1024]{1,0:T(8,128)(2,1)S(1)} all-gather(f16[64,1024]{1,0:T(8,128)(2,1)S(1)} %fusion.5), channel_id=1, replica_groups=mesh['src'=16,'tgt'=32] {'src'}, dimensions={0}, use_global_device_ids=true | all-gather | bytes 2228224 | tf_op jit(solution)/shard_map/all_gather | solution.py:153
  55.2 2.0 %fusion.1.target = bf16[1024,1024]{1,0:T(8,128)(2,1)} fusion(f16[1024,1024]{1,0:T(8,128)(2,1)S(1)} %all-gather.1), kind=kLoop, calls=%fused_computation.2 | loop fusion | flops 5242880 | bytes 4194304 | tf_op jit(solution)/shard_map/convert_element_type | solution.py:26
  57.2 0.0 all-to-all-done
  57.2 0.0 copy-done.2
  57.2 0.0 copy-done.3
  57.2 0.0 copy-start
  57.2 1.6 %copy-done = bf16[1024,1024]{1,0:T(8,128)(2,1)S(1)} copy-done((bf16[1024,1024]{1,0:T(8,128)(2,1)S(1)}, bf16[1024,1024]{1,0:T(8,128)(2,1)}, u32[]{:S(2)}) %copy-start) | copy-done | bytes 2097176
  58.8 5.9 %scores.1 = (f32[1024,1024]{1,0:T(8,128)}, f32[8,128]{1,0:T(8,128)S(1)}, f32[8,128]{1,0:T(8,128)S(1)}) custom-call(bf16[1024,1024]{1,0:T(8,128)(2,1)S(1)} %bitcast.14, bf16[1024,1024]{1,0:T(8,128)(2,1)S(1)} %copy-done, s32[8,128]{1,0:T(8,128)S(1)} %bitcast.15, s32[8,128]{1,0:T(8,128)S(1)} %bitcast.16), custom_call_target="tpu_custom_call" | custom-call | tf_op jit(solution)/shard_map/scores/pallas_call | solution.py:110
  64.7 20.8 %all_to_all.15.row_levels = f32[32,8,128]{2,1,0:T(8,128)S(1)} all-to-all(f32[32,8,128]{2,1,0:T(8,128)S(1)} %broadcast_in_dim.7), channel_id=1, replica_groups=mesh['src'=16,'tgt'=32] {'tgt'}, dimensions={0} | all-to-all | bytes 262144 | tf_op jit(solution)/shard_map/all_to_all | solution.py:156
  85.5 17.9 %all_to_all.16.col_levels = f32[16,8,128]{2,1,0:T(8,128)S(1)} all-to-all(f32[16,8,128]{2,1,0:T(8,128)S(1)} %broadcast_in_dim.8), channel_id=1, replica_groups=mesh['src'=16,'tgt'=32] {'src'}, dimensions={0} | all-to-all | bytes 131072 | tf_op jit(solution)/shard_map/all_to_all | solution.py:155
  103.4 0.0 copy-start.1
  103.4 2.2 %copy-done.1 = f32[1024,1024]{1,0:T(8,128)S(1)} copy-done((f32[1024,1024]{1,0:T(8,128)S(1)}, f32[1024,1024]{1,0:T(8,128)}, u32[]{:S(2)}) %copy-start.1) | copy-done | bytes 4194328
  105.6 5.0 %margins.1 = f32[1024,1024]{1,0:T(8,128)} custom-call(f32[1024,1024]{1,0:T(8,128)S(1)} %copy-done.1, f32[32,8,128]{2,1,0:T(8,128)S(1)} %all_to_all.15.row_levels, f32[16,8,128]{2,1,0:T(8,128)S(1)} %all_to_all.16.col_levels), custom_call_target="tpu_custom_call" | custom-call | tf_op jit(solution)/shard_map/margins/pallas_call | solution.py:132
  (2 shorter events, 0.0 us)
Async XLA Ops:
  0.0 13.0 %copy-start.4 = (bf16[1024,64]{0,1:T(8,128)(2,1)S(1)}, bf16[1024,64]{0,1:T(8,128)(2,1)}, u32[]{:S(2)}) copy-start(bf16[1024,64]{0,1:T(8,128)(2,1)} %param.5) | copy-start | bytes 393220
  2.5 54.8 %all-to-all-start = ((bf16[32,32,1024]{2,1,0:T(8,128)(2,1)}), bf16[32,32,1024]{2,1,0:T(8,128)(2,1)S(1)}, u32[]{:S(2)}, u32[]{:S(2)}) async-start(bf16[32,32,1024]{2,1,0:T(8,128)(2,1)} %broadcast_in_dim.6), calls=%async_computation | async-start | bytes 4194304 | tf_op jit(solution)/shard_map/all_to_all | solution.py:151
  13.0 44.2 %copy-start.2 = (s32[1024]{0:T(1024)S(1)}, s32[1024]{0:T(1024)}, u32[]{:S(2)}) copy-start(s32[1024]{0:T(1024)} %param.6) | copy-start | bytes 12292
  13.0 44.2 %copy-start.3 = (s32[1024]{0:T(1024)S(1)}, s32[1024]{0:T(1024)}, u32[]{:S(2)}) copy-start(s32[1024]{0:T(1024)} %param.7) | copy-start | bytes 12292
  57.2 1.6 %copy-start = (bf16[1024,1024]{1,0:T(8,128)(2,1)S(1)}, bf16[1024,1024]{1,0:T(8,128)(2,1)}, u32[]{:S(2)}) copy-start(bf16[1024,1024]{1,0:T(8,128)(2,1)} %fusion.1.target) | copy-start | bytes 6291460
  103.4 2.2 %copy-start.1 = (f32[1024,1024]{1,0:T(8,128)S(1)}, f32[1024,1024]{1,0:T(8,128)}, u32[]{:S(2)}) copy-start(f32[1024,1024]{1,0:T(8,128)} %get-tuple-element.8.scores) | copy-start | bytes 12582916

commit v3 on v2

v3 whole, which is shorter than its diff:
```python
import math

import jax
import jax.numpy as jnp
from jax import lax
from jax.experimental import pallas as pl
from jax.experimental.pallas import tpu as pltpu
from jax.sharding import PartitionSpec as P

smoothing_divisor = 256.0
floor_value = -1e30
absent_below = -1e29
eps = 1e-06
lanes = 128
code_scale = 512.0
log2_e = math.log2(math.e)


def encode(x):
    wide = x.astype(jnp.float32)
    root = jnp.sqrt(jnp.abs(wide)) * code_scale
    return jnp.where(wide < 0, -root, root).astype(jnp.float16)


def decode(code):
    wide = code.astype(jnp.float32)
    return (wide * jnp.abs(wide) * (1.0 / code_scale**2)).astype(jnp.bfloat16)


def log_sum(levels):
    highest = jnp.max(levels, axis=0)
    return highest + jnp.log2(jnp.sum(jnp.exp2(levels - highest[None]), axis=0))


def as_column(line):
    return jnp.transpose(jnp.broadcast_to(line, (lanes, lanes)))


def as_line(column):
    return jnp.transpose(jnp.broadcast_to(column, (lanes, lanes)))[:1]


def joined(lines):
    return jnp.concatenate([lines[i : i + 1, :] for i in range(lines.shape[0])], axis=1)


def level(highest, total):
    return jnp.where(highest < absent_below, floor_value, highest + jnp.log2(total))


def inverse_norm(features):
    depth, count = features.shape
    squares = jnp.zeros((8, count), jnp.float32)
    step = 64
    for k in range(0, depth, step):
        wide = features[k : k + step, :].astype(jnp.float32)
        squares += jnp.sum((wide * wide).reshape(step // 8, 8, count), axis=0)
    return lax.rsqrt(jnp.sum(squares, axis=0, keepdims=True) + eps)


def score_kernel(
    source_far, target, source_group, target_group, scores, row_out, col_out, source, turned, scale_cols, group_cols, sems
):
    depth, rows = source.shape
    columns = target.shape[1]
    size = depth // sems.shape[0]
    fetches = []
    for k in range(sems.shape[0]):
        block = slice(k * size, (k + 1) * size)
        fetches.append(pltpu.make_async_copy(source_far.at[block, :], source.at[block, :], sems.at[k]))
        fetches[-1].start()
    target_scale = inverse_norm(target)
    for i in range(rows // lanes):
        group_cols[i * lanes : (i + 1) * lanes, :] = as_column(source_group[i : i + 1, :])
    for k, fetch in enumerate(fetches):
        fetch.wait()
        block = slice(k * size, (k + 1) * size)
        for i in range(rows // lanes):
            span = slice(i * lanes, (i + 1) * lanes)
            turned[span, block] = jnp.transpose(source[block, span])
    source_scale = inverse_norm(source) * (smoothing_divisor * log2_e)
    for i in range(rows // lanes):
        span = slice(i * lanes, (i + 1) * lanes)
        scale_cols[span, :] = as_column(source_scale[:, span])

    products = jnp.dot(turned[...], target[...], preferred_element_type=jnp.float32)
    scaled = products * scale_cols[:, :1] * target_scale
    allowed = group_cols[:, :1] == joined(target_group)
    scores[...] = jnp.where(allowed, scaled, floor_value)

    col_max = jnp.max(scores[...], axis=0, keepdims=True)
    col_sum = jnp.zeros((1, columns), jnp.float32)
    row_lines = []
    for i in range(rows // lanes):
        part = scores[i * lanes : (i + 1) * lanes, :]
        row_max = jnp.max(part, axis=1, keepdims=True)
        row_sum = jnp.sum(jnp.exp2(part - row_max), axis=1, keepdims=True)
        row_lines.append(as_line(level(row_max, row_sum)))
        col_sum += jnp.sum(jnp.exp2(part - col_max), axis=0, keepdims=True)
    row_out[...] = jnp.concatenate(row_lines, axis=0)
    col_level = level(col_max, col_sum)
    col_out[...] = jnp.concatenate(
        [col_level[:, i * lanes : (i + 1) * lanes] for i in range(columns // lanes)], axis=0
    )


def margin_kernel(scores, row_levels, col_levels, margins, ready, sems):
    rows = log_sum(row_levels[...]) - 1.0
    col = joined(log_sum(col_levels[...]) - 1.0)
    copies = []
    for i in range(rows.shape[0]):
        block = slice(i * lanes, (i + 1) * lanes)
        part = scores[block, :]
        row = as_column(rows[i : i + 1, :])[:, :1]
        pair = jnp.maximum(row, col) + jnp.log2(1.0 + jnp.exp2(-jnp.abs(row - col)))
        ready[block, :] = jnp.where(part < absent_below, 0.0, (part - pair) * (1.0 / log2_e))
        copies.append(pltpu.make_async_copy(ready.at[block, :], margins.at[block, :], sems.at[i]))
        copies[-1].start()
    for copy in copies:
        copy.wait()


def spread_kernel(part, copies, sem):
    for k in range(copies.shape[0]):
        pltpu.make_async_copy(part, copies.at[k], sem).start()
    for k in range(copies.shape[0]):
        pltpu.make_async_copy(part, copies.at[k], sem).wait()


def spread(part, count):
    return pl.pallas_call(
        spread_kernel,
        out_shape=jax.ShapeDtypeStruct((count,) + part.shape, part.dtype),
        in_specs=[pl.BlockSpec(memory_space=pltpu.VMEM)],
        out_specs=pl.BlockSpec(memory_space=pltpu.HBM),
        scratch_shapes=[pltpu.SemaphoreType.DMA],
        name="spread",
    )(part)


def find_scores(source, target, src_group, tgt_group):
    rows, columns = source.shape[1], target.shape[1]
    vmem = pl.BlockSpec(memory_space=pltpu.VMEM)
    return pl.pallas_call(
        score_kernel,
        out_shape=(
            jax.ShapeDtypeStruct((rows, columns), jnp.float32),
            jax.ShapeDtypeStruct((rows // lanes, lanes), jnp.float32),
            jax.ShapeDtypeStruct((columns // lanes, lanes), jnp.float32),
        ),
        in_specs=[pl.BlockSpec(memory_space=pltpu.HBM), vmem, vmem, vmem],
        out_specs=(vmem, vmem, vmem),
        scratch_shapes=[
            pltpu.VMEM(source.shape, jnp.bfloat16),
            pltpu.VMEM((rows, source.shape[0]), jnp.bfloat16),
            pltpu.VMEM((rows, lanes), jnp.float32),
            pltpu.VMEM((rows, lanes), jnp.int32),
            pltpu.SemaphoreType.DMA((4,)),
        ],
        compiler_params=pltpu.CompilerParams(vmem_limit_bytes=20 * 2**20),
        name="scores",
    )(source, target, src_group.reshape(-1, lanes), tgt_group.reshape(-1, lanes))


def find_margins(scores, row_levels, col_levels):
    rows, columns = scores.shape
    vmem = pl.BlockSpec(memory_space=pltpu.VMEM)
    return pl.pallas_call(
        margin_kernel,
        out_shape=jax.ShapeDtypeStruct((rows, columns), jnp.float32),
        in_specs=[vmem, vmem, vmem],
        out_specs=pl.BlockSpec(memory_space=pl.ANY),
        scratch_shapes=[
            pltpu.VMEM((rows, columns), jnp.float32),
            pltpu.SemaphoreType.DMA((rows // lanes,)),
        ],
        compiler_params=pltpu.CompilerParams(vmem_limit_bytes=16 * 2**20),
        name="margins",
    )(scores, row_levels, col_levels)


def local(source_emb, target_emb, src_group, tgt_group):
    z_size = lax.axis_size("src")
    t_size = lax.axis_size("tgt")
    source = lax.all_to_all(spread(source_emb.T, t_size), "tgt", 0, 0)
    source = source.reshape(-1, source.shape[-1])
    source = pltpu.with_memory_space_constraint(source, pltpu.HBM)
    codes = lax.all_gather(encode(target_emb.T), "src", axis=0, tiled=True)
    target = decode(codes)
    scores, row_level, col_level = find_scores(source, target, src_group, tgt_group)
    col_levels = lax.all_to_all(jnp.broadcast_to(col_level[None], (z_size,) + col_level.shape), "src", 0, 0)
    row_levels = lax.all_to_all(jnp.broadcast_to(row_level[None], (t_size,) + row_level.shape), "tgt", 0, 0)
    return find_margins(scores, row_levels, col_levels)


def solution(mesh):
    in_specs = (P("src", "tgt"), P("tgt", "src"), P("src"), P("tgt"))
    out_specs = P("src", "tgt")
    return jax.shard_map(local, mesh=mesh, in_specs=in_specs, out_specs=out_specs, check_vma=False)
```

time: 111 us -> 102 us (0.919)
  local copies, waits for them, and re-layouts: 6.26 us -> 0.03 us
  other arithmetic: 2.17 us -> 0.83 us
    unnamed x10 -> x6, local copies, waits for them, and re-layouts: 3.79 us -> 0.02 us
    broadcast_in_dim x1 -> x0, local copies, waits for them, and re-layouts: 2.45 us -> none  [local(): jnp.broadcast_to(part[None], (t_size,) + part.shape)]
    convert_element_type x1, other arithmetic: 2.04 us -> 0.7 us  [decode(): return (wide * jnp.abs(wide) * (1.0 / code_scale ** 2)).astype(jnp.bfloat16)]
    pallas_call x1 -> x2, Pallas kernels: 5.02 us -> 5.21 us  [the longest x1 3.04 us: find_margins(): pl.pallas_call(margin_kernel, out_shape=jax.ShapeDtypeStruct((rows, colum...]
  transfers between devices with their start and end apart: 1 -> 1, of which waited for: 0 -> 0; matrix products, arithmetic and copies ran while one was open for 2% -> 1% of each run, Pallas kernels for 0% -> 0%
where the time goes in v3:
time: 102 us
  blocking collectives  79.6 us (78%)
  starting transfers between devices  11.2 us (11%)
  Pallas kernels  10.4 us (10%)
    all_gather x1, blocking collectives, local(): codes = lax.all_gather(encode(target_emb.T), 'src', axis=0, tiled=True)  40.9 us
    all_to_all x1, blocking collectives, local(): lax.all_to_all(jnp.broadcast_to(row_level[None], (t_size,) + row_level.sh...  21 us
    all_to_all x1, blocking collectives, local(): lax.all_to_all(jnp.broadcast_to(col_level[None], (z_size,) + col_level.sh...  17.7 us
    all_to_all x1, starting transfers between devices, local(): source = lax.all_to_all(spread(source_emb.T, t_size), 'tgt', 0, 0)  11.2 us
    pallas_call x1, Pallas kernels, find_scores(): pl.pallas_call(score_kernel, out_shape=(jax.ShapeDtypeStruct((rows, colum...  5.17 us
    pallas_call x1, Pallas kernels, find_margins(): pl.pallas_call(margin_kernel, out_shape=jax.ShapeDtypeStruct((rows, colum...  3.04 us
    pallas_call x1, Pallas kernels, spread(): pl.pallas_call(spread_kernel, out_shape=jax.ShapeDtypeStruct((count,) + p...  2.16 us
  transfers between devices with their start and end apart: 1, of which 0 were waited for; matrix products, arithmetic and copies ran while one was open for 1% of the time, Pallas kernels for 0%

profile of v3, /device:TPU:1, one launch (start us, length us, event | category | flops | bytes accessed | tf_op | source)
XLA Modules:
  0.0 102.2 jit_solution(4935241295620746114)
XLA Ops:
  0.0 0.0 copy-start.2
  0.0 2.2 %spread.1 = bf16[32,32,1024]{2,1,0:T(8,128)(2,1)} custom-call(bf16[32,1024]{1,0:T(8,128)(2,1)} %bitcast.16), custom_call_target="tpu_custom_call" | custom-call | tf_op jit(solution)/shard_map/spread/pallas_call | solution.py:131
  2.2 11.2 %all-to-all-start = ((bf16[32,32,1024]{2,1,0:T(8,128)(2,1)}), bf16[32,32,1024]{2,1,0:T(8,128)(2,1)}, u32[]{:S(2)}, u32[]{:S(2)}) async-start(bf16[32,32,1024]{2,1,0:T(8,128)(2,1)} %spread.1), calls=%async_computation | async-start | bytes 4194304 | tf_op jit(solution)/shard_map/all_to_all | solution.py:185
  13.4 0.0 copy-done.2
  13.4 0.0 copy-start
  13.4 0.0 copy-start.1
  13.4 0.1 fusion.5
  13.6 40.9 %all-gather.1 = f16[1024,1024]{1,0:T(8,128)(2,1)S(1)} all-gather(f16[64,1024]{1,0:T(8,128)(2,1)S(1)} %fusion.5), channel_id=1, replica_groups=mesh['src'=16,'tgt'=32] {'src'}, dimensions={0}, use_global_device_ids=true | all-gather | bytes 2228224 | tf_op jit(solution)/shard_map/all_gather | solution.py:188
  54.5 0.7 fusion.1.target
  55.2 0.0 all-to-all-done
  55.2 0.0 copy-done
  55.2 0.0 copy-done.1
  55.2 5.2 %scores.1 = (f32[1024,1024]{1,0:T(8,128)S(1)}, f32[8,128]{1,0:T(8,128)S(1)}, f32[8,128]{1,0:T(8,128)S(1)}) custom-call(bf16[1024,1024]{1,0:T(8,128)(2,1)} %bitcast.1.source_far, bf16[1024,1024]{1,0:T(8,128)(2,1)S(1)} %fusion.1.target, s32[8,128]{1,0:T(8,128)S(1)} %bitcast.14, s32[8,128]{1,0:T(8,128)S(1)} %bitcast.15), custom_call_target="tpu_custom_call" | custom-call | tf_op jit(solution)/shard_map/scores/pallas_call | solution.py:144
  60.4 21.0 %all_to_all.15.row_levels = f32[32,8,128]{2,1,0:T(8,128)S(1)} all-to-all(f32[32,8,128]{2,1,0:T(8,128)S(1)} %broadcast_in_dim.4), channel_id=1, replica_groups=mesh['src'=16,'tgt'=32] {'tgt'}, dimensions={0} | all-to-all | bytes 262144 | tf_op jit(solution)/shard_map/all_to_all | solution.py:192
  81.4 17.7 %all_to_all.16.col_levels = f32[16,8,128]{2,1,0:T(8,128)S(1)} all-to-all(f32[16,8,128]{2,1,0:T(8,128)S(1)} %broadcast_in_dim.5), channel_id=1, replica_groups=mesh['src'=16,'tgt'=32] {'src'}, dimensions={0} | all-to-all | bytes 131072 | tf_op jit(solution)/shard_map/all_to_all | solution.py:191
  99.1 3.0 %margins.1 = f32[1024,1024]{1,0:T(8,128)} custom-call(f32[1024,1024]{1,0:T(8,128)S(1)} %get-tuple-element.8.scores, f32[32,8,128]{2,1,0:T(8,128)S(1)} %all_to_all.15.row_levels, f32[16,8,128]{2,1,0:T(8,128)S(1)} %all_to_all.16.col_levels), custom_call_target="tpu_custom_call" | custom-call | tf_op jit(solution)/shard_map/margins/pallas_call | solution.py:168
  (2 shorter events, 0.0 us)
Async XLA Ops:
  0.0 13.4 %copy-start.2 = (bf16[1024,64]{0,1:T(8,128)(2,1)S(1)}, bf16[1024,64]{0,1:T(8,128)(2,1)}, u32[]{:S(2)}) copy-start(bf16[1024,64]{0,1:T(8,128)(2,1)} %param.5) | copy-start | bytes 393220
  2.2 53.0 %all-to-all-start = ((bf16[32,32,1024]{2,1,0:T(8,128)(2,1)}), bf16[32,32,1024]{2,1,0:T(8,128)(2,1)}, u32[]{:S(2)}, u32[]{:S(2)}) async-start(bf16[32,32,1024]{2,1,0:T(8,128)(2,1)} %spread.1), calls=%async_computation | async-start | bytes 4194304 | tf_op jit(solution)/shard_map/all_to_all | solution.py:185
  13.4 41.8 %copy-start = (s32[1024]{0:T(1024)S(1)}, s32[1024]{0:T(1024)}, u32[]{:S(2)}) copy-start(s32[1024]{0:T(1024)} %param.6) | copy-start | bytes 12292
  13.4 41.8 %copy-start.1 = (s32[1024]{0:T(1024)S(1)}, s32[1024]{0:T(1024)}, u32[]{:S(2)}) copy-start(s32[1024]{0:T(1024)} %param.7) | copy-start | bytes 12292

commit v4 on v3

--- a/solution.py
+++ b/solution.py
@@ -13,6 +13,7 @@
 eps = 1e-06
 lanes = 128
 code_scale = 512.0
+near_range = 100.0
 log2_e = math.log2(math.e)
 
 
@@ -105,19 +106,40 @@
 
 
 def margin_kernel(scores, row_levels, col_levels, margins, ready, sems):
-    rows = log_sum(row_levels[...]) - 1.0
-    col = joined(log_sum(col_levels[...]) - 1.0)
-    copies = []
-    for i in range(rows.shape[0]):
-        block = slice(i * lanes, (i + 1) * lanes)
-        part = scores[block, :]
-        row = as_column(rows[i : i + 1, :])[:, :1]
-        pair = jnp.maximum(row, col) + jnp.log2(1.0 + jnp.exp2(-jnp.abs(row - col)))
-        ready[block, :] = jnp.where(part < absent_below, 0.0, (part - pair) * (1.0 / log2_e))
-        copies.append(pltpu.make_async_copy(ready.at[block, :], margins.at[block, :], sems.at[i]))
-        copies[-1].start()
-    for copy in copies:
-        copy.wait()
+    rows = log_sum(row_levels[...])
+    cols = log_sum(col_levels[...])
+    highest = jnp.maximum(jnp.max(rows), jnp.max(cols))
+    lowest = jnp.minimum(jnp.min(rows), jnp.min(cols))
+    near = highest - lowest < near_range
+
+    def write(row_terms, col_term, pair_of):
+        copies = []
+        for i in range(rows.shape[0]):
+            block = slice(i * lanes, (i + 1) * lanes)
+            part = scores[block, :]
+            pair = pair_of(as_column(row_terms[i : i + 1, :])[:, :1], col_term)
+            ready[block, :] = jnp.where(part < absent_below, 0.0, (part - pair) * (1.0 / log2_e))
+            copies.append(pltpu.make_async_copy(ready.at[block, :], margins.at[block, :], sems.at[i]))
+            copies[-1].start()
+        for copy in copies:
+            copy.wait()
+
+    @pl.when(near)
+    def _():
+        middle = highest - 1.0
+        write(
+            jnp.exp2(rows - highest),
+            joined(jnp.exp2(cols - highest)),
+            lambda row, col: jnp.log2(row + col) + middle,
+        )
+
+    @pl.when(jnp.logical_not(near))
+    def _():
+        write(
+            rows - 1.0,
+            joined(cols - 1.0),
+            lambda row, col: jnp.maximum(row, col) + jnp.log2(1.0 + jnp.exp2(-jnp.abs(row - col))),
+        )
 
 
 def spread_kernel(part, copies, sem):

time: 102 us -> 102 us (level)
  no operation moved by 1% of the time
where the time goes in v4:
time: 102 us
  blocking collectives  79.6 us (78%)
  starting transfers between devices  11.2 us (11%)
  Pallas kernels  9.96 us (10%)
    all_gather x1, blocking collectives, local(): codes = lax.all_gather(encode(target_emb.T), 'src', axis=0, tiled=True)  40.9 us
    all_to_all x1, blocking collectives, local(): lax.all_to_all(jnp.broadcast_to(row_level[None], (t_size,) + row_level.sh...  21 us
    all_to_all x1, blocking collectives, local(): lax.all_to_all(jnp.broadcast_to(col_level[None], (z_size,) + col_level.sh...  17.7 us
    all_to_all x1, starting transfers between devices, local(): source = lax.all_to_all(spread(source_emb.T, t_size), 'tgt', 0, 0)  11.2 us
    pallas_call x1, Pallas kernels, find_scores(): pl.pallas_call(score_kernel, out_shape=(jax.ShapeDtypeStruct((rows, colum...  5.17 us
    pallas_call x1, Pallas kernels, find_margins(): pl.pallas_call(margin_kernel, out_shape=jax.ShapeDtypeStruct((rows, colum...  2.63 us
    pallas_call x1, Pallas kernels, spread(): pl.pallas_call(spread_kernel, out_shape=jax.ShapeDtypeStruct((count,) + p...  2.16 us
  transfers between devices with their start and end apart: 1, of which 0 were waited for; matrix products, arithmetic and copies ran while one was open for 1% of the time, Pallas kernels for 0%

profile of v4, /device:TPU:1, one launch (start us, length us, event | category | flops | bytes accessed | tf_op | source)
XLA Modules:
  0.0 101.8 jit_solution(4143671248384656474)
XLA Ops:
  0.0 0.0 copy-start.2
  0.0 2.2 %spread.1 = bf16[32,32,1024]{2,1,0:T(8,128)(2,1)} custom-call(bf16[32,1024]{1,0:T(8,128)(2,1)} %bitcast.16), custom_call_target="tpu_custom_call" | custom-call | tf_op jit(solution)/shard_map/spread/pallas_call | solution.py:153
  2.2 11.2 %all-to-all-start = ((bf16[32,32,1024]{2,1,0:T(8,128)(2,1)}), bf16[32,32,1024]{2,1,0:T(8,128)(2,1)}, u32[]{:S(2)}, u32[]{:S(2)}) async-start(bf16[32,32,1024]{2,1,0:T(8,128)(2,1)} %spread.1), calls=%async_computation | async-start | bytes 4194304 | tf_op jit(solution)/shard_map/all_to_all | solution.py:207
  13.4 0.0 copy-done.2
  13.4 0.0 copy-start
  13.4 0.0 copy-start.1
  13.4 0.1 fusion.5
  13.6 40.9 %all-gather.1 = f16[1024,1024]{1,0:T(8,128)(2,1)S(1)} all-gather(f16[64,1024]{1,0:T(8,128)(2,1)S(1)} %fusion.5), channel_id=1, replica_groups=mesh['src'=16,'tgt'=32] {'src'}, dimensions={0}, use_global_device_ids=true | all-gather | bytes 2228224 | tf_op jit(solution)/shard_map/all_gather | solution.py:210
  54.5 0.7 fusion.1.target
  55.2 0.0 all-to-all-done
  55.2 0.0 copy-done
  55.2 0.0 copy-done.1
  55.2 5.2 %scores.1 = (f32[1024,1024]{1,0:T(8,128)S(1)}, f32[8,128]{1,0:T(8,128)S(1)}, f32[8,128]{1,0:T(8,128)S(1)}) custom-call(bf16[1024,1024]{1,0:T(8,128)(2,1)} %bitcast.1.source_far, bf16[1024,1024]{1,0:T(8,128)(2,1)S(1)} %fusion.1.target, s32[8,128]{1,0:T(8,128)S(1)} %bitcast.14, s32[8,128]{1,0:T(8,128)S(1)} %bitcast.15), custom_call_target="tpu_custom_call" | custom-call | tf_op jit(solution)/shard_map/scores/pallas_call | solution.py:166
  60.4 21.0 %all_to_all.15.row_levels = f32[32,8,128]{2,1,0:T(8,128)S(1)} all-to-all(f32[32,8,128]{2,1,0:T(8,128)S(1)} %broadcast_in_dim.4), channel_id=1, replica_groups=mesh['src'=16,'tgt'=32] {'tgt'}, dimensions={0} | all-to-all | bytes 262144 | tf_op jit(solution)/shard_map/all_to_all | solution.py:214
  81.4 17.7 %all_to_all.16.col_levels = f32[16,8,128]{2,1,0:T(8,128)S(1)} all-to-all(f32[16,8,128]{2,1,0:T(8,128)S(1)} %broadcast_in_dim.5), channel_id=1, replica_groups=mesh['src'=16,'tgt'=32] {'src'}, dimensions={0} | all-to-all | bytes 131072 | tf_op jit(solution)/shard_map/all_to_all | solution.py:213
  99.1 2.6 %margins.1 = f32[1024,1024]{1,0:T(8,128)} custom-call(f32[1024,1024]{1,0:T(8,128)S(1)} %get-tuple-element.8.scores, f32[32,8,128]{2,1,0:T(8,128)S(1)} %all_to_all.15.row_levels, f32[16,8,128]{2,1,0:T(8,128)S(1)} %all_to_all.16.col_levels), custom_call_target="tpu_custom_call" | custom-call | tf_op jit(solution)/shard_map/margins/pallas_call | solution.py:190
  (2 shorter events, 0.0 us)
Async XLA Ops:
  0.0 13.4 %copy-start.2 = (bf16[1024,64]{0,1:T(8,128)(2,1)S(1)}, bf16[1024,64]{0,1:T(8,128)(2,1)}, u32[]{:S(2)}) copy-start(bf16[1024,64]{0,1:T(8,128)(2,1)} %param.5) | copy-start | bytes 393220
  2.2 53.0 %all-to-all-start = ((bf16[32,32,1024]{2,1,0:T(8,128)(2,1)}), bf16[32,32,1024]{2,1,0:T(8,128)(2,1)}, u32[]{:S(2)}, u32[]{:S(2)}) async-start(bf16[32,32,1024]{2,1,0:T(8,128)(2,1)} %spread.1), calls=%async_computation | async-start | bytes 4194304 | tf_op jit(solution)/shard_map/all_to_all | solution.py:207
  13.4 41.8 %copy-start = (s32[1024]{0:T(1024)S(1)}, s32[1024]{0:T(1024)}, u32[]{:S(2)}) copy-start(s32[1024]{0:T(1024)} %param.6) | copy-start | bytes 12292
  13.4 41.8 %copy-start.1 = (s32[1024]{0:T(1024)S(1)}, s32[1024]{0:T(1024)}, u32[]{:S(2)}) copy-start(s32[1024]{0:T(1024)} %param.7) | copy-start | bytes 12292

commit v5 on v4

--- a/solution.py
+++ b/solution.py
@@ -114,12 +114,14 @@
 
     def write(row_terms, col_term, pair_of):
         copies = []
-        for i in range(rows.shape[0]):
-            block = slice(i * lanes, (i + 1) * lanes)
+        size = scores.shape[0] // sems.shape[0]
+        for k in range(sems.shape[0]):
+            block = slice(k * size, (k + 1) * size)
+            i, first = divmod(k * size, lanes)
             part = scores[block, :]
-            pair = pair_of(as_column(row_terms[i : i + 1, :])[:, :1], col_term)
+            pair = pair_of(as_column(row_terms[i : i + 1, :])[first : first + size, :1], col_term)
             ready[block, :] = jnp.where(part < absent_below, 0.0, (part - pair) * (1.0 / log2_e))
-            copies.append(pltpu.make_async_copy(ready.at[block, :], margins.at[block, :], sems.at[i]))
+            copies.append(pltpu.make_async_copy(ready.at[block, :], margins.at[block, :], sems.at[k]))
             copies[-1].start()
         for copy in copies:
             copy.wait()
@@ -194,7 +196,7 @@
         out_specs=pl.BlockSpec(memory_space=pl.ANY),
         scratch_shapes=[
             pltpu.VMEM((rows, columns), jnp.float32),
-            pltpu.SemaphoreType.DMA((rows // lanes,)),
+            pltpu.SemaphoreType.DMA((16,)),
         ],
         compiler_params=pltpu.CompilerParams(vmem_limit_bytes=16 * 2**20),
         name="margins",

time: 102 us -> 102 us (level)
  no operation moved by 1% of the time
where the time goes in v5:
time: 102 us
  blocking collectives  79.6 us (78%)
  starting transfers between devices  11.2 us (11%)
  Pallas kernels  10.3 us (10%)
    all_gather x1, blocking collectives, local(): codes = lax.all_gather(encode(target_emb.T), 'src', axis=0, tiled=True)  40.9 us
    all_to_all x1, blocking collectives, local(): lax.all_to_all(jnp.broadcast_to(row_level[None], (t_size,) + row_level.sh...  21 us
    all_to_all x1, blocking collectives, local(): lax.all_to_all(jnp.broadcast_to(col_level[None], (z_size,) + col_level.sh...  17.7 us
    all_to_all x1, starting transfers between devices, local(): source = lax.all_to_all(spread(source_emb.T, t_size), 'tgt', 0, 0)  11.2 us
    pallas_call x1, Pallas kernels, find_scores(): pl.pallas_call(score_kernel, out_shape=(jax.ShapeDtypeStruct((rows, colum...  5.17 us
    pallas_call x1, Pallas kernels, find_margins(): pl.pallas_call(margin_kernel, out_shape=jax.ShapeDtypeStruct((rows, colum...  2.95 us
    pallas_call x1, Pallas kernels, spread(): pl.pallas_call(spread_kernel, out_shape=jax.ShapeDtypeStruct((count,) + p...  2.16 us
  transfers between devices with their start and end apart: 1, of which 0 were waited for; matrix products, arithmetic and copies ran while one was open for 1% of the time, Pallas kernels for 0%

profile of v5, /device:TPU:1, one launch (start us, length us, event | category | flops | bytes accessed | tf_op | source)
XLA Modules:
  0.0 102.1 jit_solution(14546160759150464969)
XLA Ops:
  0.0 0.0 copy-start.2
  0.0 2.2 %spread.1 = bf16[32,32,1024]{2,1,0:T(8,128)(2,1)} custom-call(bf16[32,1024]{1,0:T(8,128)(2,1)} %bitcast.16), custom_call_target="tpu_custom_call" | custom-call | tf_op jit(solution)/shard_map/spread/pallas_call | solution.py:155
  2.2 11.2 %all-to-all-start = ((bf16[32,32,1024]{2,1,0:T(8,128)(2,1)}), bf16[32,32,1024]{2,1,0:T(8,128)(2,1)}, u32[]{:S(2)}, u32[]{:S(2)}) async-start(bf16[32,32,1024]{2,1,0:T(8,128)(2,1)} %spread.1), calls=%async_computation | async-start | bytes 4194304 | tf_op jit(solution)/shard_map/all_to_all | solution.py:209
  13.4 0.0 copy-done.2
  13.4 0.0 copy-start
  13.4 0.0 copy-start.1
  13.4 0.1 fusion.5
  13.6 40.9 %all-gather.1 = f16[1024,1024]{1,0:T(8,128)(2,1)S(1)} all-gather(f16[64,1024]{1,0:T(8,128)(2,1)S(1)} %fusion.5), channel_id=1, replica_groups=mesh['src'=16,'tgt'=32] {'src'}, dimensions={0}, use_global_device_ids=true | all-gather | bytes 2228224 | tf_op jit(solution)/shard_map/all_gather | solution.py:212
  54.5 0.7 fusion.1.target
  55.2 0.0 all-to-all-done
  55.2 0.0 copy-done
  55.2 0.0 copy-done.1
  55.2 5.2 %scores.1 = (f32[1024,1024]{1,0:T(8,128)S(1)}, f32[8,128]{1,0:T(8,128)S(1)}, f32[8,128]{1,0:T(8,128)S(1)}) custom-call(bf16[1024,1024]{1,0:T(8,128)(2,1)} %bitcast.1.source_far, bf16[1024,1024]{1,0:T(8,128)(2,1)S(1)} %fusion.1.target, s32[8,128]{1,0:T(8,128)S(1)} %bitcast.14, s32[8,128]{1,0:T(8,128)S(1)} %bitcast.15), custom_call_target="tpu_custom_call" | custom-call | tf_op jit(solution)/shard_map/scores/pallas_call | solution.py:168
  60.4 21.0 %all_to_all.15.row_levels = f32[32,8,128]{2,1,0:T(8,128)S(1)} all-to-all(f32[32,8,128]{2,1,0:T(8,128)S(1)} %broadcast_in_dim.4), channel_id=1, replica_groups=mesh['src'=16,'tgt'=32] {'tgt'}, dimensions={0} | all-to-all | bytes 262144 | tf_op jit(solution)/shard_map/all_to_all | solution.py:216
  81.4 17.7 %all_to_all.16.col_levels = f32[16,8,128]{2,1,0:T(8,128)S(1)} all-to-all(f32[16,8,128]{2,1,0:T(8,128)S(1)} %broadcast_in_dim.5), channel_id=1, replica_groups=mesh['src'=16,'tgt'=32] {'src'}, dimensions={0} | all-to-all | bytes 131072 | tf_op jit(solution)/shard_map/all_to_all | solution.py:215
  99.1 3.0 %margins.1 = f32[1024,1024]{1,0:T(8,128)} custom-call(f32[1024,1024]{1,0:T(8,128)S(1)} %get-tuple-element.8.scores, f32[32,8,128]{2,1,0:T(8,128)S(1)} %all_to_all.15.row_levels, f32[16,8,128]{2,1,0:T(8,128)S(1)} %all_to_all.16.col_levels), custom_call_target="tpu_custom_call" | custom-call | tf_op jit(solution)/shard_map/margins/pallas_call | solution.py:192
  (2 shorter events, 0.0 us)
Async XLA Ops:
  0.0 13.4 %copy-start.2 = (bf16[1024,64]{0,1:T(8,128)(2,1)S(1)}, bf16[1024,64]{0,1:T(8,128)(2,1)}, u32[]{:S(2)}) copy-start(bf16[1024,64]{0,1:T(8,128)(2,1)} %param.5) | copy-start | bytes 393220
  2.2 53.0 %all-to-all-start = ((bf16[32,32,1024]{2,1,0:T(8,128)(2,1)}), bf16[32,32,1024]{2,1,0:T(8,128)(2,1)}, u32[]{:S(2)}, u32[]{:S(2)}) async-start(bf16[32,32,1024]{2,1,0:T(8,128)(2,1)} %spread.1), calls=%async_computation | async-start | bytes 4194304 | tf_op jit(solution)/shard_map/all_to_all | solution.py:209
  13.4 41.8 %copy-start = (s32[1024]{0:T(1024)S(1)}, s32[1024]{0:T(1024)}, u32[]{:S(2)}) copy-start(s32[1024]{0:T(1024)} %param.6) | copy-start | bytes 12292
  13.4 41.8 %copy-start.1 = (s32[1024]{0:T(1024)S(1)}, s32[1024]{0:T(1024)}, u32[]{:S(2)}) copy-start(s32[1024]{0:T(1024)} %param.7) | copy-start | bytes 12292
